TPU v7x, 128 devices: a whole 4x4x4 slice. The times are simulated.
128 devices in a mesh: lat: 8 (over x, y_lo), lon: 16 (over z, y_hi, core).
Axes of the slice: x: 4, y: 4 (y_hi: 2, y_lo: 2; y = y_hi * 2 + y_lo), z: 4, core: 2. Of those that a mesh axis runs over, the one named last changes fastest.
Arguments:
- latents: float32 [4, 144, 192, 512], P(None, 'lat', 'lon'), may hold values from -80 to 80
- qkv_weight: bfloat16 [512, 1536], replicated, may hold values from -0.35 to 0.35
- proj_weight: bfloat16 [512, 512], replicated, may hold values from -0.25 to 0.25
- up_weight: bfloat16 [512, 2048], replicated, may hold values from -0.25 to 0.25
- down_weight: bfloat16 [2048, 512], replicated, may hold values from -0.125 to 0.125
- modulation: float32 [2, 2, 512], replicated, may hold values from -2.5 to 2.5
Outputs:
- updated: float32 [4, 144, 192, 512], P(None, 'lat', 'lon')
All inputs are finite; a program needn't handle non-finite values.
Results may differ from a plain program's by a relative error of at most 0.0045.
Values may be sent and summed in bfloat16 or wider, within the bound.
A program may use at most 128 MiB of HBM per device.

v0:
```python
import functools
import math

import jax
import jax.numpy as jnp
import numpy as np
from jax import lax
from jax.experimental import pallas as pl
from jax.experimental.pallas import tpu as pltpu
from jax.sharding import PartitionSpec as P

HEADS = 16
D = 512
FFH = 2048
UNROLL = 4
HID = 512
NEG = -1e30
BF = jnp.bfloat16
F32 = jnp.float32
MESH = pl.DeviceIdType.MESH
SLOT = {1: 0, 2: 1, 3: 2, 0: 3}
CLASSES = ((3, 6), (9, 6), (15, 3), (0, 3))


@functools.cache
def tables():
    pa = np.zeros((96, 96), np.float32)
    count = [0] * 4
    for h in range(2):
        for i in range(12):
            for lev in range(4):
                slot = SLOT[lev]
                pa[slot * 24 + count[slot], h * 48 + i * 4 + lev] = 1
                count[slot] += 1
    ps = np.zeros((288, 320), np.float32)
    count = [0] * 4
    for piece in range(4):
        for i in range(18):
            for lev in range(4):
                slot = SLOT[lev]
                ps[slot * 72 + count[slot], piece * 80 + i * 4 + lev] = 1
                count[slot] += 1
    bf = jnp.bfloat16
    return pa.astype(bf), pa.T.astype(bf), ps.astype(bf), ps.T.astype(bf)


def dot(a, b):
    return jnp.dot(a, b, preferred_element_type=F32)


def norm_mod(v, mod):
    mean = jnp.sum(v, axis=-1, keepdims=True) * (1.0 / D)
    c = v - mean
    var = jnp.sum(c * c, axis=-1, keepdims=True) * (1.0 / D)
    return (c * lax.rsqrt(var + 1e-5)) * (1.0 + mod[0:1]) + mod[1:2]


def gelu(u):
    return 0.5 * u * (1.0 + lax.erf(u * (1.0 / math.sqrt(2.0))))


def kernel(
    nlat, nlon,
    lat_hbm, wqkv_hbm, wproj_hbm, wup_hbm, wdown_hbm, mod_hbm,
    pa_hbm, pat_hbm, ps_hbm, pst_hbm,
    out_hbm,
    x, wqkv, wproj, wup, wdown, mod, pa, pat, ps, pst,
    send_a, send_s, own_a, own_c, recv_a, recv_s,
    qkv0, q1, kv1, ctx, keep_a, keep_c, back_a, back_s, home_a, home_s, n2,
    in_sem, w_sem, out_sem, ss, rs,
):
    d, j = lax.axis_index("lat"), lax.axis_index("lon")
    up_d, dn_d = lax.rem(d + 1, nlat), lax.rem(d + nlat - 1, nlat)
    rt, lf = lax.rem(j + 1, nlon), lax.rem(j + nlon - 1, nlon)
    barrier = pltpu.get_barrier_semaphore()
    for who in ((d, rt), (d, lf), (up_d, j), (dn_d, j), (up_d, rt), (dn_d, lf)):
        pl.semaphore_signal(barrier, inc=1, device_id=who, device_id_type=MESH)

    mod_cp = pltpu.make_async_copy(mod_hbm, mod, w_sem.at[0])
    mod_cp.start()
    near, far = 1 - lax.rem(j, 2), lax.rem(j, 2)

    def load(k, r0, n):
        return [pltpu.make_async_copy(
            lat_hbm.at[pl.ds(r0, n), :, p], x.at[pl.ds(r0, n), :, pl.ds(4 * p, 4)],
            in_sem.at[k, p]) for p in range(2)]

    loads = [load(far, 3 + 6 * far, 6), load(near, 3 + 6 * near, 6), load(2, 15, 3), load(3, 0, 3)]
    for cs in loads:
        for c in cs:
            c.start()
    wcp = []
    for i, (a, b) in enumerate((
        (pa_hbm, pa), (wqkv_hbm, wqkv), (pat_hbm, pat), (ps_hbm, ps), (pst_hbm, pst),
        (wproj_hbm, wproj), (wup_hbm, wup), (wdown_hbm, wdown),
    )):
        wcp.append(pltpu.make_async_copy(a, b, w_sem.at[i + 1]))
        wcp[-1].start()

    def remote(src, dst, n, who):
        return pltpu.make_async_remote_copy(
            src_ref=src, dst_ref=dst, send_sem=ss.at[n], recv_sem=rs.at[n],
            device_id=who, device_id_type=MESH)

    left, down, corner = (d, lf), (dn_d, j), (dn_d, lf)
    right, above, across = (d, rt), (up_d, j), (up_d, rt)

    def fwd_pair(k):
        return remote(send_a.at[k], recv_a.at[k], k, (d, jnp.where(k == 0, lf, rt)))

    def ret_pair(k):
        return remote(back_a.at[k], home_a.at[k], 5 + k, (d, jnp.where(k == 0, rt, lf)))

    fwd = [
        remote(send_s.at[0], recv_s.at[0], 2, left),
        remote(send_s.at[1], recv_s.at[1], 3, down),
        remote(send_s.at[2], recv_s.at[2], 4, corner),
    ]
    ret = [
        remote(back_s.at[0], home_s.at[0], 7, right),
        remote(back_s.at[1], home_s.at[1], 8, above),
        remote(back_s.at[2], home_s.at[2], 9, across),
    ]

    mod_cp.wait()

    def part(r, h):
        return x[r, pl.ds(3 * h, 3)].reshape(24, D)

    def norm_parts(rows, h):
        v = norm_mod(jnp.concatenate([part(r, h) for r in rows], axis=0), mod[0])
        if len(rows) == 3:
            v = jnp.concatenate([v, jnp.zeros((8, D), F32)], axis=0)
        return v.astype(BF)

    def fill(dst, k, h):
        for m in range(3):
            r = 3 + 6 * k + 2 * m
            dst[k, pl.ds(48 * m, 48)] = norm_parts((r, r + 1), h)

    for k, cs in ((far, loads[0]), (near, loads[1])):
        for c in cs:
            c.wait()
        fill(send_a, k, k)
        if k is far:
            pl.semaphore_wait(barrier, 6)
        fwd_pair(k).start()
    fill(own_a, far, near)
    for c in loads[3]:
        c.wait()
    send_s[2] = norm_parts((0, 1, 2), 0)
    fwd[2].start()
    send_s[1] = norm_parts((0, 1, 2), 1)
    fwd[1].start()
    for c in loads[2]:
        c.wait()
    send_s[0] = norm_parts((15, 16, 17), 0)
    fwd[0].start()
    own_c[...] = norm_parts((15, 16, 17), 1)
    fill(own_a, near, far)

    scale = math.log2(math.e) / math.sqrt(D // HEADS)
    lane = lax.broadcasted_iota(jnp.int32, (1, 128), 1)
    inside = [(lane >= 32 * h) & (lane < 32 * h + 32) for h in range(4)]
    cut = jnp.where(d == nlat - 1, NEG, 0.0)

    def apart(n):
        a = lax.rem(lax.broadcasted_iota(jnp.int32, (n, n), 0), 72) < 36
        b = lax.rem(lax.broadcasted_iota(jnp.int32, (n, n), 1), 72) < 36
        return jnp.where(a != b, cut, 0.0)

    def heads(q, kk, v, bias):
        n = kk.shape[0]
        q4 = jnp.concatenate([q * inside[h].astype(F32).astype(q.dtype) for h in range(4)], axis=0)
        s4 = lax.dot_general(q4.astype(BF), kk, (((1,), (1,)), ((), ())), preferred_element_type=F32)
        p4 = []
        for h in range(4):
            s = s4[n * h:n * h + n]
            if bias is not None:
                s = s + bias
            p4.append(jnp.exp2(s - jnp.max(s, axis=-1, keepdims=True)))
        o4 = dot(jnp.concatenate(p4, axis=0).astype(BF),
                 jnp.concatenate([v, jnp.ones((n, 128), BF)], axis=1))
        top, low = o4[:n, :128], o4[:n, 128:]
        for h in range(1, 4):
            top = jnp.where(inside[h], o4[n * h:n * h + n, :128], top)
            low = jnp.where(inside[h], o4[n * h:n * h + n, 128:], low)
        return top * (1.0 / low)

    def attend(masked):
        def step(i, carry):
            cols = [pl.ds(pl.multiple_of(512 * m + i * 128, 128), 128) for m in range(3)]
            ctx[pl.ds(0, 144), cols[0]] = heads(
                *[qkv0[:, c] for c in cols], apart(144) if masked else None)
            for m in range(2):
                ctx[pl.ds(144 + 72 * m, 72), cols[0]] = heads(
                    q1[pl.ds(72 * m, 72), cols[0]], *[kv1[m, pl.ds(0, 72), c] for c in cols[:2]],
                    apart(72) if masked else None)
            return carry

        lax.fori_loop(0, 4, step, 0, unroll=UNROLL)

    def project_in(rows):
        for c in range(3):
            cols = slice(c * D, (c + 1) * D)
            y = dot(rows, wqkv[:, cols])
            if c == 0:
                y = y * scale
            qkv0[:, cols] = y[:144].astype(BF)
            if c == 0:
                q1[...] = y[144:]
            else:
                for m in range(2):
                    kv1[m, pl.ds(0, 72), slice((c - 1) * D, c * D)] = y[144 + 72 * m:216 + 72 * m].astype(BF)

    wcp[0].wait()
    wcp[1].wait()
    for k in (far, near):
        fwd_pair(k).wait_recv()
        t = [dot(pa[...], jnp.concatenate(
            [own_a[k, pl.ds(48 * m, 48)], recv_a[k, pl.ds(48 * m, 48)]], axis=0)) for m in range(3)]
        project_in(jnp.concatenate(
            [t[m][24 * s:24 * s + 24] for s in range(4) for m in range(3)], axis=0).astype(BF))
        attend(False)
        if k is far:
            wcp[2].wait()
        for m in range(3):
            t = dot(pat[...], jnp.concatenate(
                [ctx[pl.ds(72 * s + 24 * m, 24)] for s in range(4)], axis=0).astype(BF))
            keep_a[k, pl.ds(48 * m, 48)] = t[:48].astype(BF)
            back_a[k, pl.ds(48 * m, 48)] = t[48:].astype(BF)
        ret_pair(k).start()
    for c in fwd:
        c.wait_recv()
    wcp[3].wait()
    wcp[4].wait()
    project_in(dot(ps[...], jnp.concatenate(
        [own_c[...], recv_s[0], recv_s[1], recv_s[2]], axis=0)).astype(BF))
    attend(True)
    t = dot(pst[...], ctx[...].astype(BF))
    for m in (2, 1, 0):
        back_s[m] = t[80 * m + 80:80 * m + 160].astype(BF)
        ret[m].start()
    keep_c[...] = t[:80].astype(BF)

    for n in range(5, 8):
        wcp[n].wait()
    outs = []

    def finish(pieces, context):
        attn = dot(context, wproj[...])
        for k in range(0, 12, 2):
            mid = jnp.concatenate([part(r, h) + attn[o:o + 24] for r, h, o in pieces[k:k + 2]], axis=0)
            for m in range(2):
                r, h, _ = pieces[k + m]
                x[r, pl.ds(3 * h, 3)] = mid[24 * m:24 * m + 24].reshape(3, 8, D)
            n2[pl.ds(24 * k, 48)] = norm_mod(mid, mod[1]).astype(BF)
        total = None
        for c in range(FFH // HID):
            u = dot(n2[...], wup[:, c * HID:(c + 1) * HID])
            more = dot(gelu(u).astype(BF), wdown[c * HID:(c + 1) * HID])
            total = more if total is None else total + more
        for k, (r, h, _) in enumerate(pieces):
            x[r, pl.ds(3 * h, 3)] = (part(r, h) + total[24 * k:24 * k + 24]).reshape(3, 8, D)

    def write(k, r0, n):
        for p in range(2):
            outs.append(pltpu.make_async_copy(
                x.at[pl.ds(r0, n), :, pl.ds(4 * p, 4)], out_hbm.at[pl.ds(r0, n), :, p],
                out_sem.at[k, p]))
            outs[-1].start()

    for k in (near, far):
        ret_pair(k).wait_recv()
        r0 = 3 + 6 * k
        finish([(r0 + i, h, o + 24 * i) for h, o in ((k, 0), (1 - k, 144)) for i in range(6)],
               jnp.concatenate([home_a[k], keep_a[k]], axis=0))
        write(k, r0, 6)
    for c in ret:
        c.wait_recv()
    finish([(r0 + i, h, o + 24 * i) for r0, h, o in ((15, 1, 0), (15, 0, 80), (0, 1, 160), (0, 0, 240))
            for i in range(3)],
           jnp.concatenate([keep_c[...], home_s[0], home_s[1], home_s[2]], axis=0))
    write(2, 15, 3)
    write(3, 0, 3)
    for c in outs:
        c.wait()
    for c in [fwd_pair(0), fwd_pair(1), ret_pair(0), ret_pair(1)] + fwd + ret:
        c.wait_send()


def hand_over(a, b, buf, sems):
    steps = [pl.ds(3 * i, 3) for i in range(6)]
    first = [pltpu.make_async_copy(a.at[t], buf.at[t], sems.at[0, i]) for i, t in enumerate(steps)]
    second = [pltpu.make_async_copy(buf.at[t], b.at[t], sems.at[1, i]) for i, t in enumerate(steps)]
    for c in first:
        c.start()
    for c, e in zip(first, second):
        c.wait()
        e.start()
    for e in second:
        e.wait()


def solution(mesh):
    nlat, nlon = mesh.shape["lat"], mesh.shape["lon"]

    def local(latents, qkv_weight, proj_weight, up_weight, down_weight, modulation):
        consts = tables()
        vm = pltpu.VMEM
        view = latents.transpose(1, 2, 0, 3).reshape(18, 6, 2, 4, D)
        scratch = [
            vm((18, 6, 8, D), F32), vm((D, 3 * D), BF), vm((D, D), BF), vm((D, FFH), BF),
            vm((FFH, D), BF), vm((2, 2, D), F32),
            *[vm(c.shape, BF) for c in consts],
            vm((2, 144, D), BF), vm((3, 80, D), BF), vm((2, 144, D), BF),
            vm((80, D), BF), vm((2, 144, D), BF), vm((3, 80, D), BF),
            vm((144, 3 * D), BF), vm((144, D), F32), vm((2, 80, 2 * D), BF), vm((288, D), F32), vm((2, 144, D), BF),
            vm((80, D), BF),
            vm((2, 144, D), BF), vm((3, 80, D), BF), vm((2, 144, D), BF), vm((3, 80, D), BF),
            vm((288, D), BF),
            pltpu.SemaphoreType.DMA((4, 2)), pltpu.SemaphoreType.DMA((9,)),
            pltpu.SemaphoreType.DMA((4, 2)), pltpu.SemaphoreType.DMA((10,)),
            pltpu.SemaphoreType.DMA((10,)),
        ]
        out = pl.pallas_call(
            functools.partial(kernel, nlat, nlon),
            out_shape=jax.ShapeDtypeStruct(view.shape, F32),
            in_specs=[pl.BlockSpec(memory_space=pl.ANY)] * (6 + len(consts)),
            out_specs=pl.BlockSpec(memory_space=pl.ANY),
            scratch_shapes=scratch,
            compiler_params=pltpu.CompilerParams(
                collective_id=0, has_side_effects=True, vmem_limit_bytes=62 << 20),
        )(view, qkv_weight, proj_weight, up_weight, down_weight, modulation,
          *[jnp.asarray(c) for c in consts])
        out = pl.pallas_call(
            hand_over,
            out_shape=jax.ShapeDtypeStruct(view.shape, F32),
            in_specs=[pl.BlockSpec(memory_space=pl.ANY)],
            out_specs=pl.BlockSpec(memory_space=pl.ANY),
            scratch_shapes=[vm(view.shape, F32), pltpu.SemaphoreType.DMA((2, 6))],
            compiler_params=pltpu.CompilerParams(vmem_limit_bytes=62 << 20),
        )(out)
        return out.reshape(18, 12, 4, D).transpose(2, 0, 1, 3)

    placed = (P(None, "lat", "lon", None), P(), P(), P(), P(), P())
    return jax.shard_map(
        local, mesh=mesh, in_specs=placed, out_specs=P(None, "lat", "lon", None), check_vma=False)
```

profile of v0, /device:TPU:0, one launch (start us, length us, event | category | flops | bytes accessed | tf_op | source)
XLA Modules:
  0.0 33.4 jit_solution(9581811294323590374)
XLA Ops:
  0.0 31.1 %shard_map.100.a = f32[18,6,2,4,512]{4,3,2,1,0:T(4,128)} custom-call(f32[18,6,2,4,512]{4,3,2,1,0:T(4,128)} %bitcast.6, bf16[512,1536]{1,0:T(8,128)(2,1)} %wqkv_hbm.1, bf16[512,512]{1,0:T(8,128)(2,1)} %wproj_hbm.1, bf16[512,2048]{1,0:T(8,128)(2,1)} %wup_hbm.1, bf16[2048,512]{1,0:T(8,128)(2,1)} %wdown_hbm.1, f32[2,2,512]{2,1,0:T(2,128)} %mod_hbm.1, ...), custom_call_target="tpu_custom_call" | custom-call | tf_op jit(solution)/shard_map/pallas_call | solution.py:326
  31.2 2.3 %shard_map.101 = f32[18,6,2,4,512]{4,3,2,1,0:T(4,128)} custom-call(f32[18,6,2,4,512]{4,3,2,1,0:T(4,128)} %shard_map.100.a), custom_call_target="tpu_custom_call" | custom-call | tf_op jit(solution)/shard_map/pallas_call | solution.py:336
where the time goes:
time: 33.6 us; the launch traced here: 33.4 us
  Pallas kernels  33.4 us (99%)
    pallas_call x1, Pallas kernels, local(): pl.pallas_call(functools.partial(kernel, nlat, nlon), out_shape=jax.Shape...  31.1 us
    pallas_call x1, Pallas kernels, local(): pl.pallas_call(hand_over, out_shape=jax.ShapeDtypeStruct(view.shape, F32)...  2.27 us

commit v1 on v0

--- a/solution.py
+++ b/solution.py
@@ -13,6 +13,7 @@
 D = 512
 FFH = 2048
 UNROLL = 4
+VM = 60
 HID = 512
 NEG = -1e30
 BF = jnp.bfloat16
@@ -63,29 +64,30 @@
     nlat, nlon,
     lat_hbm, wqkv_hbm, wproj_hbm, wup_hbm, wdown_hbm, mod_hbm,
     pa_hbm, pat_hbm, ps_hbm, pst_hbm,
-    out_hbm,
-    x, wqkv, wproj, wup, wdown, mod, pa, pat, ps, pst,
+    x,
+    wqkv, wproj, wup, wdown, mod, pa, pat, ps, pst,
     send_a, send_s, own_a, own_c, recv_a, recv_s,
     qkv0, q1, kv1, ctx, keep_a, keep_c, back_a, back_s, home_a, home_s, n2,
-    in_sem, w_sem, out_sem, ss, rs,
+    in_sem, w_sem, ss, rs,
 ):
     d, j = lax.axis_index("lat"), lax.axis_index("lon")
     up_d, dn_d = lax.rem(d + 1, nlat), lax.rem(d + nlat - 1, nlat)
     rt, lf = lax.rem(j + 1, nlon), lax.rem(j + nlon - 1, nlon)
     barrier = pltpu.get_barrier_semaphore()
-    for who in ((d, rt), (d, lf), (up_d, j), (dn_d, j), (up_d, rt), (dn_d, lf)):
+    for who in ((d, rt), (d, lf), (up_d, j), (dn_d, j), (up_d, lf), (dn_d, rt)):
         pl.semaphore_signal(barrier, inc=1, device_id=who, device_id_type=MESH)
 
     mod_cp = pltpu.make_async_copy(mod_hbm, mod, w_sem.at[0])
     mod_cp.start()
     near, far = 1 - lax.rem(j, 2), lax.rem(j, 2)
 
-    def load(k, r0, n):
+    def load(n, r0, count, h):
         return [pltpu.make_async_copy(
-            lat_hbm.at[pl.ds(r0, n), :, p], x.at[pl.ds(r0, n), :, pl.ds(4 * p, 4)],
-            in_sem.at[k, p]) for p in range(2)]
-
-    loads = [load(far, 3 + 6 * far, 6), load(near, 3 + 6 * near, 6), load(2, 15, 3), load(3, 0, 3)]
+            lat_hbm.at[pl.ds(r0, count), pl.ds(3 * h, 3), p],
+            x.at[pl.ds(r0, count), pl.ds(3 * h, 3), pl.ds(4 * p, 4)], in_sem.at[n, p]) for p in range(2)]
+
+    loads = [load(0, 3 + 6 * far, 6, far), load(1, 3 + 6 * near, 6, near), load(2, 3 + 6 * far, 6, near),
+             load(3, 3 + 6 * near, 6, far), load(4, 15, 3, 0), load(5, 15, 3, 1), load(6, 0, 3, 0), load(7, 0, 3, 1)]
     for cs in loads:
         for c in cs:
             c.start()
@@ -102,8 +104,7 @@
             src_ref=src, dst_ref=dst, send_sem=ss.at[n], recv_sem=rs.at[n],
             device_id=who, device_id_type=MESH)
 
-    left, down, corner = (d, lf), (dn_d, j), (dn_d, lf)
-    right, above, across = (d, rt), (up_d, j), (up_d, rt)
+    right, left, down, above = (d, rt), (d, lf), (dn_d, j), (up_d, j)
 
     def fwd_pair(k):
         return remote(send_a.at[k], recv_a.at[k], k, (d, jnp.where(k == 0, lf, rt)))
@@ -112,14 +113,14 @@
         return remote(back_a.at[k], home_a.at[k], 5 + k, (d, jnp.where(k == 0, rt, lf)))
 
     fwd = [
-        remote(send_s.at[0], recv_s.at[0], 2, left),
+        remote(send_s.at[0], recv_s.at[0], 2, right),
         remote(send_s.at[1], recv_s.at[1], 3, down),
-        remote(send_s.at[2], recv_s.at[2], 4, corner),
+        remote(send_s.at[2], recv_s.at[2], 4, (dn_d, rt)),
     ]
     ret = [
-        remote(back_s.at[0], home_s.at[0], 7, right),
+        remote(back_s.at[0], home_s.at[0], 7, left),
         remote(back_s.at[1], home_s.at[1], 8, above),
-        remote(back_s.at[2], home_s.at[2], 9, across),
+        remote(back_s.at[2], home_s.at[2], 9, (up_d, lf)),
     ]
 
     mod_cp.wait()
@@ -145,19 +146,19 @@
         if k is far:
             pl.semaphore_wait(barrier, 6)
         fwd_pair(k).start()
-    fill(own_a, far, near)
-    for c in loads[3]:
-        c.wait()
-    send_s[2] = norm_parts((0, 1, 2), 0)
-    fwd[2].start()
-    send_s[1] = norm_parts((0, 1, 2), 1)
-    fwd[1].start()
     for c in loads[2]:
         c.wait()
-    send_s[0] = norm_parts((15, 16, 17), 0)
-    fwd[0].start()
-    own_c[...] = norm_parts((15, 16, 17), 1)
-    fill(own_a, near, far)
+    fill(own_a, far, near)
+
+    def send_rest():
+        for cs in loads[3:]:
+            for c in cs:
+                c.wait()
+        send_s[2] = norm_parts((0, 1, 2), 1)
+        send_s[1] = norm_parts((0, 1, 2), 0)
+        send_s[0] = norm_parts((15, 16, 17), 1)
+
+    send_rest()
 
     scale = math.log2(math.e) / math.sqrt(D // HEADS)
     lane = lax.broadcasted_iota(jnp.int32, (1, 128), 1)
@@ -213,6 +214,31 @@
                 for m in range(2):
                     kv1[m, pl.ds(0, 72), slice((c - 1) * D, c * D)] = y[144 + 72 * m:216 + 72 * m].astype(BF)
 
+
+    def finish(pieces, context):
+        attn = dot(context, wproj[...])
+        count = len(pieces)
+        for k in range(0, count, 2):
+            pair = pieces[k:k + 2]
+            mid = jnp.concatenate([part(r, h) + attn[o:o + 24] for r, h, o in pair], axis=0)
+            for m, (r, h, _) in enumerate(pair):
+                x[r, pl.ds(3 * h, 3)] = mid[24 * m:24 * m + 24].reshape(3, 8, D)
+            v = norm_mod(mid, mod[1])
+            if len(pair) == 1:
+                v = jnp.concatenate([v, jnp.zeros((8, D), F32)], axis=0)
+            n2[pl.ds(24 * k, v.shape[0])] = v.astype(BF)
+        rows = pl.ds(0, 24 * count + 8 * (count % 2))
+        total = None
+        for c in range(FFH // HID):
+            u = dot(n2[rows], wup[:, c * HID:(c + 1) * HID])
+            more = dot(gelu(u).astype(BF), wdown[c * HID:(c + 1) * HID])
+            total = more if total is None else total + more
+        for k, (r, h, _) in enumerate(pieces):
+            x[r, pl.ds(3 * h, 3)] = (part(r, h) + total[24 * k:24 * k + 24]).reshape(3, 8, D)
+
+    def span(k, h, o):
+        return [(3 + 6 * k + i, h, o + 24 * i) for i in range(6)]
+
     wcp[0].wait()
     wcp[1].wait()
     for k in (far, near):
@@ -223,6 +249,9 @@
             [t[m][24 * s:24 * s + 24] for s in range(4) for m in range(3)], axis=0).astype(BF))
         attend(False)
         if k is far:
+            for c in (fwd[2], fwd[1], fwd[0]):
+                c.start()
+        if k is far:
             wcp[2].wait()
         for m in range(3):
             t = dot(pat[...], jnp.concatenate(
@@ -230,6 +259,12 @@
             keep_a[k, pl.ds(48 * m, 48)] = t[:48].astype(BF)
             back_a[k, pl.ds(48 * m, 48)] = t[48:].astype(BF)
         ret_pair(k).start()
+        if k is far:
+            own_c[...] = norm_parts((15, 16, 17), 0)
+            fill(own_a, near, far)
+            for n in range(5, 8):
+                wcp[n].wait()
+            finish(span(far, near, 0), keep_a[far])
     for c in fwd:
         c.wait_recv()
     wcp[3].wait()
@@ -243,63 +278,27 @@
         ret[m].start()
     keep_c[...] = t[:80].astype(BF)
 
-    for n in range(5, 8):
-        wcp[n].wait()
-    outs = []
-
-    def finish(pieces, context):
-        attn = dot(context, wproj[...])
-        for k in range(0, 12, 2):
-            mid = jnp.concatenate([part(r, h) + attn[o:o + 24] for r, h, o in pieces[k:k + 2]], axis=0)
-            for m in range(2):
-                r, h, _ = pieces[k + m]
-                x[r, pl.ds(3 * h, 3)] = mid[24 * m:24 * m + 24].reshape(3, 8, D)
-            n2[pl.ds(24 * k, 48)] = norm_mod(mid, mod[1]).astype(BF)
-        total = None
-        for c in range(FFH // HID):
-            u = dot(n2[...], wup[:, c * HID:(c + 1) * HID])
-            more = dot(gelu(u).astype(BF), wdown[c * HID:(c + 1) * HID])
-            total = more if total is None else total + more
-        for k, (r, h, _) in enumerate(pieces):
-            x[r, pl.ds(3 * h, 3)] = (part(r, h) + total[24 * k:24 * k + 24]).reshape(3, 8, D)
-
-    def write(k, r0, n):
-        for p in range(2):
-            outs.append(pltpu.make_async_copy(
-                x.at[pl.ds(r0, n), :, pl.ds(4 * p, 4)], out_hbm.at[pl.ds(r0, n), :, p],
-                out_sem.at[k, p]))
-            outs[-1].start()
-
-    for k in (near, far):
-        ret_pair(k).wait_recv()
-        r0 = 3 + 6 * k
-        finish([(r0 + i, h, o + 24 * i) for h, o in ((k, 0), (1 - k, 144)) for i in range(6)],
-               jnp.concatenate([home_a[k], keep_a[k]], axis=0))
-        write(k, r0, 6)
+    ret_pair(near).wait_recv()
+    finish(span(near, near, 0) + span(near, far, 144), jnp.concatenate([home_a[near], keep_a[near]], axis=0))
+    ret_pair(far).wait_recv()
+    finish(span(far, far, 0) + [(15 + i, 0, 144 + 24 * i) for i in range(3)],
+           jnp.concatenate([home_a[far], keep_c[...]], axis=0))
     for c in ret:
         c.wait_recv()
-    finish([(r0 + i, h, o + 24 * i) for r0, h, o in ((15, 1, 0), (15, 0, 80), (0, 1, 160), (0, 0, 240))
-            for i in range(3)],
-           jnp.concatenate([keep_c[...], home_s[0], home_s[1], home_s[2]], axis=0))
-    write(2, 15, 3)
-    write(3, 0, 3)
-    for c in outs:
-        c.wait()
+    finish([(r0 + i, h, o + 24 * i) for r0, h, o in ((15, 1, 0), (0, 0, 80), (0, 1, 160)) for i in range(3)],
+           jnp.concatenate([home_s[0], home_s[1], home_s[2]], axis=0))
     for c in [fwd_pair(0), fwd_pair(1), ret_pair(0), ret_pair(1)] + fwd + ret:
         c.wait_send()
 
 
-def hand_over(a, b, buf, sems):
-    steps = [pl.ds(3 * i, 3) for i in range(6)]
-    first = [pltpu.make_async_copy(a.at[t], buf.at[t], sems.at[0, i]) for i, t in enumerate(steps)]
-    second = [pltpu.make_async_copy(buf.at[t], b.at[t], sems.at[1, i]) for i, t in enumerate(steps)]
-    for c in first:
+def hand_over(a, b, sems):
+    copies = [pltpu.make_async_copy(
+        a.at[pl.ds(3 * i, 3), :, pl.ds(4 * p, 4)], b.at[pl.ds(3 * i, 3), :, p], sems.at[i, p])
+        for i in range(6) for p in range(2)]
+    for c in copies:
         c.start()
-    for c, e in zip(first, second):
+    for c in copies:
         c.wait()
-        e.start()
-    for e in second:
-        e.wait()
 
 
 def solution(mesh):
@@ -310,7 +309,7 @@
         vm = pltpu.VMEM
         view = latents.transpose(1, 2, 0, 3).reshape(18, 6, 2, 4, D)
         scratch = [
-            vm((18, 6, 8, D), F32), vm((D, 3 * D), BF), vm((D, D), BF), vm((D, FFH), BF),
+            vm((D, 3 * D), BF), vm((D, D), BF), vm((D, FFH), BF),
             vm((FFH, D), BF), vm((2, 2, D), F32),
             *[vm(c.shape, BF) for c in consts],
             vm((2, 144, D), BF), vm((3, 80, D), BF), vm((2, 144, D), BF),
@@ -319,27 +318,27 @@
             vm((80, D), BF),
             vm((2, 144, D), BF), vm((3, 80, D), BF), vm((2, 144, D), BF), vm((3, 80, D), BF),
             vm((288, D), BF),
-            pltpu.SemaphoreType.DMA((4, 2)), pltpu.SemaphoreType.DMA((9,)),
-            pltpu.SemaphoreType.DMA((4, 2)), pltpu.SemaphoreType.DMA((10,)),
+            pltpu.SemaphoreType.DMA((8, 2)), pltpu.SemaphoreType.DMA((9,)),
+            pltpu.SemaphoreType.DMA((10,)),
             pltpu.SemaphoreType.DMA((10,)),
         ]
         out = pl.pallas_call(
             functools.partial(kernel, nlat, nlon),
-            out_shape=jax.ShapeDtypeStruct(view.shape, F32),
+            out_shape=pltpu.VMEM((18, 6, 8, D), F32),
             in_specs=[pl.BlockSpec(memory_space=pl.ANY)] * (6 + len(consts)),
-            out_specs=pl.BlockSpec(memory_space=pl.ANY),
+            out_specs=pl.BlockSpec(memory_space=pltpu.VMEM),
             scratch_shapes=scratch,
             compiler_params=pltpu.CompilerParams(
-                collective_id=0, has_side_effects=True, vmem_limit_bytes=62 << 20),
+                collective_id=0, has_side_effects=True, vmem_limit_bytes=VM << 20),
         )(view, qkv_weight, proj_weight, up_weight, down_weight, modulation,
           *[jnp.asarray(c) for c in consts])
         out = pl.pallas_call(
             hand_over,
             out_shape=jax.ShapeDtypeStruct(view.shape, F32),
-            in_specs=[pl.BlockSpec(memory_space=pl.ANY)],
+            in_specs=[pl.BlockSpec(memory_space=pltpu.VMEM)],
             out_specs=pl.BlockSpec(memory_space=pl.ANY),
-            scratch_shapes=[vm(view.shape, F32), pltpu.SemaphoreType.DMA((2, 6))],
-            compiler_params=pltpu.CompilerParams(vmem_limit_bytes=62 << 20),
+            scratch_shapes=[pltpu.SemaphoreType.DMA((6, 2))],
+            compiler_params=pltpu.CompilerParams(vmem_limit_bytes=16 << 20),
         )(out)
         return out.reshape(18, 12, 4, D).transpose(2, 0, 1, 3)
 

time: 33.6 us -> 30.2 us (0.90)
  Pallas kernels: 33.4 us -> 30 us
    pallas_call x1, Pallas kernels: 31.1 us -> 28.7 us  [local(): pl.pallas_call(functools.partial(kernel, nlat, nlon), out_shape=pltpu.VME...]
    pallas_call x1, Pallas kernels: 2.27 us -> 1.3 us  [local(): pl.pallas_call(hand_over, out_shape=jax.ShapeDtypeStruct(view.shape, F32)...]
where the time goes in v1:
time: 30.2 us; the launch traced here: 30 us
  Pallas kernels  30 us (99%)
    pallas_call x1, Pallas kernels, local(): pl.pallas_call(functools.partial(kernel, nlat, nlon), out_shape=pltpu.VME...  28.7 us
    pallas_call x1, Pallas kernels, local(): pl.pallas_call(hand_over, out_shape=jax.ShapeDtypeStruct(view.shape, F32)...  1.3 us

profile of v1, /device:TPU:0, one launch (start us, length us, event | category | flops | bytes accessed | tf_op | source)
XLA Modules:
  0.0 30.0 jit_solution(3240393387817612837)
XLA Ops:
  0.0 28.7 %shard_map.100.a = f32[18,6,8,512]{3,2,1,0:T(8,128)S(1)} custom-call(f32[18,6,2,4,512]{4,3,2,1,0:T(4,128)} %bitcast.6, bf16[512,1536]{1,0:T(8,128)(2,1)} %wqkv_hbm.1, bf16[512,512]{1,0:T(8,128)(2,1)} %wproj_hbm.1, bf16[512,2048]{1,0:T(8,128)(2,1)} %wup_hbm.1, bf16[2048,512]{1,0:T(8,128)(2,1)} %wdown_hbm.1, f32[2,2,512]{2,1,0:T(2,128)} %mod_hbm.1, ...), custom_call_target="tpu_custom_call" | custom-call | tf_op jit(solution)/shard_map/pallas_call | solution.py:325
  28.7 1.3 %shard_map.101 = f32[18,6,2,4,512]{4,3,2,1,0:T(4,128)} custom-call(f32[18,6,8,512]{3,2,1,0:T(8,128)S(1)} %shard_map.100.a), custom_call_target="tpu_custom_call" | custom-call | tf_op jit(solution)/shard_map/pallas_call | solution.py:335

commit v2 on v1

--- a/solution.py
+++ b/solution.py
@@ -139,26 +139,24 @@
             r = 3 + 6 * k + 2 * m
             dst[k, pl.ds(48 * m, 48)] = norm_parts((r, r + 1), h)
 
-    for k, cs in ((far, loads[0]), (near, loads[1])):
-        for c in cs:
+    for n, r0, h, dst in ((7, 0, 1, 2), (6, 0, 0, 1), (5, 15, 1, 0)):
+        for c in loads[n]:
             c.wait()
-        fill(send_a, k, k)
-        if k is far:
-            pl.semaphore_wait(barrier, 6)
-        fwd_pair(k).start()
+        send_s[dst] = norm_parts((r0, r0 + 1, r0 + 2), h)
+    pl.semaphore_wait(barrier, 6)
+    for c in (fwd[2], fwd[1], fwd[0]):
+        c.start()
+    for c in loads[0]:
+        c.wait()
+    fill(send_a, far, far)
+    fwd_pair(far).start()
+    for c in loads[1]:
+        c.wait()
+    fill(send_a, near, near)
+    fwd_pair(near).start()
     for c in loads[2]:
         c.wait()
     fill(own_a, far, near)
-
-    def send_rest():
-        for cs in loads[3:]:
-            for c in cs:
-                c.wait()
-        send_s[2] = norm_parts((0, 1, 2), 1)
-        send_s[1] = norm_parts((0, 1, 2), 0)
-        send_s[0] = norm_parts((15, 16, 17), 1)
-
-    send_rest()
 
     scale = math.log2(math.e) / math.sqrt(D // HEADS)
     lane = lax.broadcasted_iota(jnp.int32, (1, 128), 1)
@@ -239,32 +237,28 @@
     def span(k, h, o):
         return [(3 + 6 * k + i, h, o + 24 * i) for i in range(6)]
 
-    wcp[0].wait()
-    wcp[1].wait()
-    for k in (far, near):
+    def pair_step(k):
         fwd_pair(k).wait_recv()
         t = [dot(pa[...], jnp.concatenate(
             [own_a[k, pl.ds(48 * m, 48)], recv_a[k, pl.ds(48 * m, 48)]], axis=0)) for m in range(3)]
         project_in(jnp.concatenate(
             [t[m][24 * s:24 * s + 24] for s in range(4) for m in range(3)], axis=0).astype(BF))
         attend(False)
-        if k is far:
-            for c in (fwd[2], fwd[1], fwd[0]):
-                c.start()
-        if k is far:
-            wcp[2].wait()
         for m in range(3):
             t = dot(pat[...], jnp.concatenate(
                 [ctx[pl.ds(72 * s + 24 * m, 24)] for s in range(4)], axis=0).astype(BF))
             keep_a[k, pl.ds(48 * m, 48)] = t[:48].astype(BF)
             back_a[k, pl.ds(48 * m, 48)] = t[48:].astype(BF)
         ret_pair(k).start()
-        if k is far:
-            own_c[...] = norm_parts((15, 16, 17), 0)
-            fill(own_a, near, far)
-            for n in range(5, 8):
-                wcp[n].wait()
-            finish(span(far, near, 0), keep_a[far])
+
+    for n in range(3):
+        wcp[n].wait()
+    pair_step(far)
+    for n in (3, 4):
+        for c in loads[n]:
+            c.wait()
+    own_c[...] = norm_parts((15, 16, 17), 0)
+    fill(own_a, near, far)
     for c in fwd:
         c.wait_recv()
     wcp[3].wait()
@@ -278,15 +272,19 @@
         ret[m].start()
     keep_c[...] = t[:80].astype(BF)
 
+    pair_step(near)
+    for n in range(5, 8):
+        wcp[n].wait()
     ret_pair(near).wait_recv()
-    finish(span(near, near, 0) + span(near, far, 144), jnp.concatenate([home_a[near], keep_a[near]], axis=0))
-    ret_pair(far).wait_recv()
-    finish(span(far, far, 0) + [(15 + i, 0, 144 + 24 * i) for i in range(3)],
-           jnp.concatenate([home_a[far], keep_c[...]], axis=0))
+    finish(span(near, near, 0) + span(near, far, 144) + span(far, near, 288),
+           jnp.concatenate([home_a[near], keep_a[near], keep_a[far]], axis=0))
     for c in ret:
         c.wait_recv()
     finish([(r0 + i, h, o + 24 * i) for r0, h, o in ((15, 1, 0), (0, 0, 80), (0, 1, 160)) for i in range(3)],
            jnp.concatenate([home_s[0], home_s[1], home_s[2]], axis=0))
+    ret_pair(far).wait_recv()
+    finish(span(far, far, 0) + [(15 + i, 0, 144 + 24 * i) for i in range(3)],
+           jnp.concatenate([home_a[far], keep_c[...]], axis=0))
     for c in [fwd_pair(0), fwd_pair(1), ret_pair(0), ret_pair(1)] + fwd + ret:
         c.wait_send()
 
@@ -317,7 +315,7 @@
             vm((144, 3 * D), BF), vm((144, D), F32), vm((2, 80, 2 * D), BF), vm((288, D), F32), vm((2, 144, D), BF),
             vm((80, D), BF),
             vm((2, 144, D), BF), vm((3, 80, D), BF), vm((2, 144, D), BF), vm((3, 80, D), BF),
-            vm((288, D), BF),
+            vm((432, D), BF),
             pltpu.SemaphoreType.DMA((8, 2)), pltpu.SemaphoreType.DMA((9,)),
             pltpu.SemaphoreType.DMA((10,)),
             pltpu.SemaphoreType.DMA((10,)),

time: 30.2 us -> 29.2 us (0.967)
  Pallas kernels: 30 us -> 29.1 us
    pallas_call x1, Pallas kernels: 28.7 us -> 27.8 us  [local(): pl.pallas_call(functools.partial(kernel, nlat, nlon), out_shape=pltpu.VME...]
where the time goes in v2:
time: 29.2 us; the launch traced here: 29.1 us
  Pallas kernels  29.1 us (100%)
    pallas_call x1, Pallas kernels, local(): pl.pallas_call(functools.partial(kernel, nlat, nlon), out_shape=pltpu.VME...  27.8 us
    pallas_call x1, Pallas kernels, local(): pl.pallas_call(hand_over, out_shape=jax.ShapeDtypeStruct(view.shape, F32)...  1.3 us

profile of v2, /device:TPU:0, one launch (start us, length us, event | category | flops | bytes accessed | tf_op | source)
XLA Modules:
  0.0 29.1 jit_solution(5651347168466062334)
XLA Ops:
  0.0 27.8 %shard_map.100.a = f32[18,6,8,512]{3,2,1,0:T(8,128)S(1)} custom-call(f32[18,6,2,4,512]{4,3,2,1,0:T(4,128)} %bitcast.6, bf16[512,1536]{1,0:T(8,128)(2,1)} %wqkv_hbm.1, bf16[512,512]{1,0:T(8,128)(2,1)} %wproj_hbm.1, bf16[512,2048]{1,0:T(8,128)(2,1)} %wup_hbm.1, bf16[2048,512]{1,0:T(8,128)(2,1)} %wdown_hbm.1, f32[2,2,512]{2,1,0:T(2,128)} %mod_hbm.1, ...), custom_call_target="tpu_custom_call" | custom-call | tf_op jit(solution)/shard_map/pallas_call | solution.py:323
  27.8 1.3 %shard_map.101 = f32[18,6,2,4,512]{4,3,2,1,0:T(4,128)} custom-call(f32[18,6,8,512]{3,2,1,0:T(8,128)S(1)} %shard_map.100.a), custom_call_target="tpu_custom_call" | custom-call | tf_op jit(solution)/shard_map/pallas_call | solution.py:333

commit v3 on v2

--- a/solution.py
+++ b/solution.py
@@ -14,7 +14,7 @@
 FFH = 2048
 UNROLL = 4
 VM = 60
-HID = 512
+HID = 1024
 NEG = -1e30
 BF = jnp.bfloat16
 F32 = jnp.float32

time: 29.2 us -> 29 us (level)
  no operation moved by 1% of the time
where the time goes in v3:
time: 29 us; the launch traced here: 28.9 us
  Pallas kernels  28.9 us (100%)
    pallas_call x1, Pallas kernels, local(): pl.pallas_call(functools.partial(kernel, nlat, nlon), out_shape=pltpu.VME...  27.5 us
    pallas_call x1, Pallas kernels, local(): pl.pallas_call(hand_over, out_shape=jax.ShapeDtypeStruct(view.shape, F32)...  1.3 us

profile of v3, /device:TPU:0, one launch (start us, length us, event | category | flops | bytes accessed | tf_op | source)
XLA Modules:
  0.0 28.9 jit_solution(9812440808032991360)
XLA Ops:
  0.0 27.5 %shard_map.100.a = f32[18,6,8,512]{3,2,1,0:T(8,128)S(1)} custom-call(f32[18,6,2,4,512]{4,3,2,1,0:T(4,128)} %bitcast.6, bf16[512,1536]{1,0:T(8,128)(2,1)} %wqkv_hbm.1, bf16[512,512]{1,0:T(8,128)(2,1)} %wproj_hbm.1, bf16[512,2048]{1,0:T(8,128)(2,1)} %wup_hbm.1, bf16[2048,512]{1,0:T(8,128)(2,1)} %wdown_hbm.1, f32[2,2,512]{2,1,0:T(2,128)} %mod_hbm.1, ...), custom_call_target="tpu_custom_call" | custom-call | tf_op jit(solution)/shard_map/pallas_call | solution.py:323
  27.6 1.3 %shard_map.101 = f32[18,6,2,4,512]{4,3,2,1,0:T(4,128)} custom-call(f32[18,6,8,512]{3,2,1,0:T(8,128)S(1)} %shard_map.100.a), custom_call_target="tpu_custom_call" | custom-call | tf_op jit(solution)/shard_map/pallas_call | solution.py:333
